TPU v7x, 32 devices: a whole 2x2x4 slice. The times are simulated.
32 devices in a mesh: seq: 4 (over y, x), dp: 8 (over z, core).
Axes of the slice: x: 2, y: 2, z: 4, core: 2. Of those that a mesh axis runs over, the one named last changes fastest.
Arguments:
- video_qkv: bfloat16 [8, 512, 3, 2048], P('dp', 'seq'), may hold values from -6 to 6
- video_cotangent: bfloat16 [8, 512, 2048], P('dp', 'seq'), may hold values from -192 to 192
- prompt_states: bfloat16 [8, 128, 4096], P('dp', None, 'seq'), may hold values from -6 to 6
- text_weight: bfloat16 [4096, 6144], P('seq', 'dp'), may hold values from -0.09375 to 0.09375
- text_cotangent: bfloat16 [8, 128, 2048], P('dp', None, 'seq'), may hold values from -192 to 192
- gain_query: float32 [16, 128], P('seq'), may hold values from 0.25 to 1.75
- gain_key: float32 [16, 128], P('seq'), may hold values from 0.25 to 1.75
- prompt_lengths: int32 [8], P('dp'), may hold values from 16 to 128
- prompt_source: int32 [8], replicated, may hold values from 0 to 7, each once
Outputs:
- grad_video_qkv: bfloat16 [8, 512, 3, 2048], P('dp', 'seq')
- grad_text_qkv: bfloat16 [8, 128, 6144], P('dp', None, 'seq')
Inputs may be any that keep to these rules, and one draw needn't show every extreme that they name: prompt_source is a permutation: every row of prompt_states is the prompt of exactly one clip. Clip c's valid prompt rows are its first prompt_lengths[c] rows.
All inputs are finite; a program needn't handle non-finite values.
Results may differ from a plain program's by a relative error of at most 0.0091.
Values may be sent and summed in bfloat16 or wider, within the bound.
A program may use at most 64 MiB of HBM per device.

v0:
```python
import math

import jax
import jax.numpy as jnp
from jax import lax
from jax.sharding import PartitionSpec as P

EPS = 1e-06


def rms_scale(values, gain):
    return values * lax.rsqrt(jnp.mean(values * values, axis=-1, keepdims=True) + EPS) * gain


def block_grads(query_normed, key_normed, values, upstream, key_valid):
    scale = 1.0 / math.sqrt(query_normed.shape[-1])
    scores = jnp.dot(query_normed, key_normed.T, preferred_element_type=jnp.float32) * scale
    weights = jnp.exp(scores) * key_valid
    probs = weights / jnp.sum(weights, axis=-1, keepdims=True)
    probs_low = probs.astype(jnp.bfloat16)
    grad_probs = jnp.dot(upstream, values.T, preferred_element_type=jnp.float32)
    delta = jnp.sum(probs * grad_probs, axis=-1, keepdims=True)
    grad_scores = (probs * (grad_probs - delta) * scale).astype(jnp.bfloat16)
    grad_query = jnp.dot(grad_scores, key_normed, preferred_element_type=jnp.float32)
    grad_key = jnp.dot(grad_scores.T, query_normed, preferred_element_type=jnp.float32)
    grad_value = jnp.dot(probs_low.T, upstream, preferred_element_type=jnp.float32)
    return (grad_query, grad_key, grad_value)


def norm_grad(raw, gain, cotangent):
    unused, pull = jax.vjp(lambda inner: rms_scale(inner, gain), raw)
    return pull(cotangent)[0]


def pick_block(source, piece):
    hits = jnp.arange(piece.shape[0], dtype=jnp.int32) == source
    shape = (piece.shape[0],) + (1,) * (piece.ndim - 1)
    chosen = jnp.sum(jnp.where(hits.reshape(shape), piece, jnp.zeros_like(piece)), axis=0)
    return chosen


def head_grads(inputs, key_valid, block_rows, tokens):
    video_part, up_video, text_part, up_text, gain_q, gain_k = inputs
    head_size = video_part.shape[-1]
    query_raw = jnp.concatenate([video_part[0], text_part[0].T], 0).astype(jnp.float32)
    key_raw = jnp.concatenate([video_part[1], text_part[1].T], 0).astype(jnp.float32)
    values = jnp.concatenate([video_part[2], text_part[2].T], 0)
    upstream = jnp.concatenate([up_video, up_text], 0)
    query_normed = rms_scale(query_raw, gain_q).astype(jnp.bfloat16)
    key_normed = rms_scale(key_raw, gain_k).astype(jnp.bfloat16)
    blocks = tokens // block_rows
    query_blocks = query_normed[:tokens].reshape(blocks, block_rows, head_size)
    upstream_blocks = upstream[:tokens].reshape(blocks, block_rows, head_size)

    def step(totals, pair):
        grad_qn, grad_kn, grad_value = block_grads(pair[0], key_normed, values, pair[1], key_valid)
        return ((totals[0] + grad_kn, totals[1] + grad_value), grad_qn)

    zeros = jnp.zeros(key_raw.shape, jnp.float32)
    (sum_key, sum_value), grad_video_rows = lax.scan(
        step, (zeros, zeros), (query_blocks, upstream_blocks)
    )
    grad_text_rows, text_key, text_value = block_grads(
        query_normed[tokens:], key_normed, values, upstream[tokens:], key_valid
    )
    grad_qn = jnp.concatenate([grad_video_rows.reshape(tokens, head_size), grad_text_rows], 0)
    grad_query = norm_grad(query_raw, gain_q, grad_qn)
    grad_key = norm_grad(key_raw, gain_k, sum_key + text_key)
    return jnp.stack([grad_query, grad_key, sum_value + text_value], 0).astype(jnp.bfloat16)


def shards(
    video_qkv,
    video_cotangent,
    prompt_states,
    text_weight,
    text_cotangent,
    gain_query,
    gain_key,
    prompt_lengths,
    prompt_source,
):
    clip = lax.axis_index("dp")
    source = lax.dynamic_index_in_dim(prompt_source, clip, 0, keepdims=False)
    local_heads, head_size = gain_query.shape
    heads = video_qkv.shape[3] // head_size
    tok_dev = video_qkv.shape[1]
    prompt = prompt_states.shape[1]
    rows_mine = local_heads * 3 * head_size
    full_weight = lax.all_gather(text_weight, "dp", axis=1, tiled=True)
    encoder_rows = prompt_states[0]
    text_local = lax.psum_scatter(
        lax.dot_general(
            full_weight, encoder_rows, (((0,), (1,)), ((), ())), preferred_element_type=jnp.float32
        ),
        "seq",
        scatter_dimension=0,
        tiled=True,
    ).astype(jnp.bfloat16)
    text_local = pick_block(source, lax.all_gather(text_local[None], "dp", axis=0, tiled=True))
    text_heads = text_local.reshape(local_heads, 3, head_size, prompt)
    video_local = video_qkv[0].reshape(tok_dev, 3, heads, head_size)
    upstream_local = video_cotangent[0].reshape(tok_dev, 1, heads, head_size)
    video_mixed, upstream_mixed = (
        lax.all_to_all(video_local, "seq", split_axis=2, concat_axis=0, tiled=True),
        lax.all_to_all(upstream_local, "seq", split_axis=2, concat_axis=0, tiled=True),
    )
    tokens = video_mixed.shape[0]
    video_heads = jnp.transpose(video_mixed, (2, 1, 0, 3))
    upstream_heads = jnp.transpose(upstream_mixed[:, 0], (1, 0, 2))
    upstream_text = jnp.transpose(
        text_cotangent[0].reshape(prompt, local_heads, head_size), (1, 0, 2)
    )
    key_valid = jnp.concatenate(
        [
            jnp.ones((tokens,), jnp.float32),
            (jnp.arange(prompt, dtype=jnp.int32) < prompt_lengths[0]).astype(jnp.float32),
        ]
    )
    block_rows = min(512, tokens)
    grads = lax.map(
        lambda inputs: head_grads(inputs, key_valid, block_rows, tokens),
        (video_heads, upstream_heads, text_heads, upstream_text, gain_query, gain_key),
    )
    video_grad = jnp.transpose(grads[:, :, :tokens], (2, 1, 0, 3))
    video_back = lax.all_to_all(video_grad, "seq", split_axis=0, concat_axis=2, tiled=True)
    grad_video_qkv = video_back.reshape(1, tok_dev, 3, heads * head_size)
    grad_text_qkv = jnp.transpose(grads[:, :, tokens:], (2, 0, 1, 3)).reshape(1, prompt, rows_mine)
    return (grad_video_qkv, grad_text_qkv)


def solution(mesh):
    in_specs = (
        P("dp", "seq", None, None),
        P("dp", "seq", None),
        P("dp", None, "seq"),
        P("seq", "dp"),
        P("dp", None, "seq"),
        P("seq", None),
        P("seq", None),
        P("dp"),
        P(),
    )
    out_specs = (P("dp", "seq", None, None), P("dp", None, "seq"))
    return jax.shard_map(shards, mesh=mesh, in_specs=in_specs, out_specs=out_specs, check_vma=False)
```

profile of v0, /device:TPU:0, one launch (start us, length us, event | category | flops | bytes accessed | tf_op | source)
XLA Modules:
  0.0 298.1 jit_solution(6900126690467720188)
XLA Ops:
  7.2 0.7 all-gather.4.cloned.1.call-update
  8.0 121.1 %all-gather.4.cloned.1.call-done = bf16[1024,6144]{1,0:T(8,128)(2,1)} async-done(((bf16[1024,768]{1,0:T(8,128)(2,1)}), bf16[1024,6144]{1,0:T(8,128)(2,1)}) %all-gather.4.cloned.1.call-update) | async-done | bytes 12582928 | tf_op jit(solution)/shard_map/all_gather | solution.py:90
  129.1 9.7 %fusion.54 = f32[6144,128]{1,0:T(8,128)} fusion(bf16[1024,6144]{1,0:T(8,128)(2,1)} %all-gather.4.cloned.1.call-done, bf16[1,128,1024]{2,1,0:T(8,128)(2,1)S(1)} %copy-done), kind=kOutput, calls=%fused_computation.90 | convolution fusion | flops 1610612736 | bytes 15990784 | tf_op jit(solution)/shard_map/dot_general | solution.py:93
  138.9 42.3 %reduce-scatter.2.cloned.1.call-done = f32[1536,128]{1,0:T(8,128)} async-done(((f32[6144,128]{1,0:T(8,128)}), f32[1536,128]{1,0:T(8,128)}) %reduce-scatter.2.cloned.1.call-update) | async-done | bytes 786448 | tf_op jit(solution)/shard_map/reduce_scatter | solution.py:92
  181.1 1.9 convert_element_type.55
  183.1 1.0 copy.62
  184.1 3.5 %all-to-all-start.1 = ((bf16[128,1,16,128]{0,3,1,2:T(8,128)(2,1)}), bf16[128,1,16,128]{0,3,1,2:T(8,128)(2,1)S(1)}, u32[]{:S(2)}, u32[]{:S(2)}) async-start(bf16[128,1,16,128]{0,3,1,2:T(8,128)(2,1)} %bitcast.34), calls=%async_computation.2 | async-start | bytes 1048576 | tf_op jit(solution)/shard_map/all_to_all | solution.py:106
  187.6 1.9 copy.58
  189.5 1.2 copy.59
  190.7 5.1 %all-to-all-done.1 = bf16[128,1,16,128]{0,3,1,2:T(8,128)(2,1)S(1)} async-done(((bf16[128,1,16,128]{0,3,1,2:T(8,128)(2,1)}), bf16[128,1,16,128]{0,3,1,2:T(8,128)(2,1)S(1)}, u32[]{:S(2)}, u32[]{:S(2)}) %all-to-all-start.1) | async-done | bytes 524320 | tf_op jit(solution)/shard_map/all_to_all | solution.py:106
  195.8 0.8 copy-done.3
  196.6 3.7 %all-to-all-start = ((bf16[128,3,16,128]{0,3,1,2:T(8,128)(2,1)}), bf16[128,3,16,128]{0,3,1,2:T(8,128)(2,1)S(1)}, u32[]{:S(2)}, u32[]{:S(2)}) async-start(bf16[128,3,16,128]{0,3,1,2:T(8,128)(2,1)} %copy.59), calls=%async_computation | async-start | bytes 3145728 | tf_op jit(solution)/shard_map/all_to_all | solution.py:105
  201.2 0.6 dynamic_slice.32
  201.8 0.6 iota_compare_fusion.1
  202.4 1.3 copy.64
  203.7 0.8 copy.65
  204.6 14.3 %all-to-all-done = bf16[128,3,16,128]{0,3,1,2:T(8,128)(2,1)S(1)} async-done(((bf16[128,3,16,128]{0,3,1,2:T(8,128)(2,1)}), bf16[128,3,16,128]{0,3,1,2:T(8,128)(2,1)S(1)}, u32[]{:S(2)}, u32[]{:S(2)}) %all-to-all-start) | async-done | bytes 1572896 | tf_op jit(solution)/shard_map/all_to_all | solution.py:105
  218.9 0.9 copy.77
  219.8 1.8 all-gather.6.cloned.1.call-done
  221.6 2.6 select_reduce_fusion
  224.3 36.1 %while.12 = (s32[]{:T(128)}, bf16[4,3,640,128]{3,2,1,0:T(8,128)(2,1)}, bf16[4,3,512,128]{3,2,1,0:T(8,128)(2,1)S(1)}, bf16[4,3,128,128]{3,2,1,0:T(8,128)(2,1)S(1)...) while((s32[]{:T(128)}, ...), condition=%wide.region_11.12_spmd, body=%wide.region_2.11_spmd.sunk | while | flops 538712320 | bytes 33646840 | solution.py:121
  224.5 0.9 copy-done.1
  225.8 0.7 fusion.101
  226.7 0.6 fusion.106
  227.4 0.4 multiply_reduce_fusion.4
  228.2 0.4 fusion.114
  228.6 0.4 fusion.108
  231.3 0.5 fusion.107
  232.1 0.8 maximum_dynamic-update-slice_fusion.2
  232.9 0.4 copy-done.2
  233.5 0.9 copy-done.1
  234.9 0.7 fusion.101
  235.7 0.6 fusion.106
  236.4 0.5 multiply_reduce_fusion.4
  237.2 0.4 fusion.114
  237.6 0.4 fusion.108
  240.3 0.5 fusion.107
  241.1 0.8 maximum_dynamic-update-slice_fusion.2
  241.9 0.4 copy-done.2
  242.5 0.9 copy-done.1
  243.9 0.7 fusion.101
  244.8 0.6 fusion.106
  245.4 0.5 multiply_reduce_fusion.4
  246.2 0.4 fusion.114
  249.3 0.5 fusion.107
  250.1 0.8 maximum_dynamic-update-slice_fusion.2
  250.9 0.4 copy-done.2
  251.6 0.9 copy-done.1
  252.9 0.7 fusion.101
  253.8 0.6 fusion.106
  254.5 0.5 multiply_reduce_fusion.4
  255.2 0.4 fusion.114
  258.3 0.5 fusion.107
  259.1 0.8 maximum_dynamic-update-slice_fusion.2
  260.0 0.4 copy-done.2
  260.4 3.1 %copy.70 = bf16[4,3,640,128]{3,0,1,2:T(4,128)(2,1)S(1)} copy(bf16[4,3,640,128]{3,2,1,0:T(8,128)(2,1)} %get-tuple-element.76) | data formatting | bytes 3932160 | tf_op jit(solution)/shard_map/while | solution.py:121
  263.4 1.7 slice_bitcast_fusion
  265.1 3.7 %all-to-all-start.2 = ((bf16[512,3,4,128]{3,2,1,0:T(4,128)(2,1)}), bf16[512,3,4,128]{3,2,1,0:T(4,128)(2,1)S(1)}, u32[]{:S(2)}, u32[]{:S(2)}) async-start(bf16[512,3,4,128]{3,2,1,0:T(4,128)(2,1)} %slice_bitcast_fusion), calls=%async_computation.3 | async-start | bytes 3145728 | tf_op jit(solution)/shard_map/all_to_all | solution.py:126
  268.8 4.0 %copy.72 = bf16[4,3,640,128]{2,3,1,0:T(8,128)(2,1)} copy(bf16[4,3,640,128]{3,2,1,0:T(8,128)(2,1)} %get-tuple-element.76) | data formatting | bytes 3932160 | tf_op jit(solution)/shard_map/while | solution.py:121
  272.8 1.0 slice.41
  273.8 0.9 copy.73
  274.7 13.9 %all-to-all-done.2 = bf16[512,3,4,128]{3,2,1,0:T(4,128)(2,1)S(1)} async-done(((bf16[512,3,4,128]{3,2,1,0:T(4,128)(2,1)}), bf16[512,3,4,128]{3,2,1,0:T(4,128)(2,1)S(1)}, u32[]{:S(2)}, u32[]{:S(2)}) %all-to-all-start.2) | async-done | bytes 1572896 | tf_op jit(solution)/shard_map/all_to_all | solution.py:126
  288.6 0.5 copy.71
  289.1 2.4 reshape.325
  (114 shorter events, 15.9 us)
Async XLA Ops:
  7.2 121.9 %copy-start = (bf16[1,128,1024]{2,1,0:T(8,128)(2,1)S(1)}, bf16[1,128,1024]{2,1,0:T(8,128)(2,1)}, u32[]{:S(2)}) copy-start(bf16[1,128,1024]{2,1,0:T(8,128)(2,1)} %param.13) | copy-start | bytes 786436
  7.2 121.9 %all-gather.4.cloned.1.call-start = ((), (), s32[]{:S(2)}) async-start(), calls=%async_computation.4 | async-start | bytes 14155776 | tf_op jit(solution)/shard_map/all_gather | solution.py:90
  7.9 173.2 %reduce-scatter.2.cloned.1.call-start = ((), (), s32[]{:S(2)}) async-start(), calls=%async_computation.5 | async-start | bytes 3932160 | tf_op jit(solution)/shard_map/reduce_scatter | solution.py:92
  138.8 44.3 %copy-start.4 = (bf16[1,128,2048]{2,1,0:T(8,128)(2,1)S(1)}, bf16[1,128,2048]{2,1,0:T(8,128)(2,1)}, u32[]{:S(2)}) copy-start(bf16[1,128,2048]{2,1,0:T(8,128)(2,1)} %param.12) | copy-start | bytes 1572868
  138.8 82.8 %all-gather.6.cloned.1.call-start = ((), (), s32[]{:S(2)}) async-start(), calls=%async_computation.6 | async-start | bytes 3538944 | tf_op jit(solution)/shard_map/all_gather | solution.py:100
  184.1 11.7 %all-to-all-start.1 = ((bf16[128,1,16,128]{0,3,1,2:T(8,128)(2,1)}), bf16[128,1,16,128]{0,3,1,2:T(8,128)(2,1)S(1)}, u32[]{:S(2)}, u32[]{:S(2)}) async-start(bf16[128,1,16,128]{0,3,1,2:T(8,128)(2,1)} %bitcast.34), calls=%async_computation.2 | async-start | bytes 1048576 | tf_op jit(solution)/shard_map/all_to_all | solution.py:106
  190.7 9.6 %copy-start.6 = (bf16[1,128,512]{2,1,0:T(8,128)(2,1)S(1)}, bf16[1,128,512]{2,1,0:T(8,128)(2,1)}, u32[]{:S(2)}) copy-start(bf16[1,128,512]{2,1,0:T(8,128)(2,1)} %param.15) | copy-start | bytes 393220
  190.7 10.4 %copy-start.7 = (s32[8]{0:T(128)S(1)}, s32[8]{0:T(128)}, u32[]{:S(2)}) copy-start(s32[8]{0:T(128)} %param.19) | copy-start | bytes 100
  195.8 0.8 copy-start.3
  196.6 22.3 %all-to-all-start = ((bf16[128,3,16,128]{0,3,1,2:T(8,128)(2,1)}), bf16[128,3,16,128]{0,3,1,2:T(8,128)(2,1)S(1)}, u32[]{:S(2)}, u32[]{:S(2)}) async-start(bf16[128,3,16,128]{0,3,1,2:T(8,128)(2,1)} %copy.59), calls=%async_computation | async-start | bytes 3145728 | tf_op jit(solution)/shard_map/all_to_all | solution.py:105
  221.6 2.6 copy-start.5
  224.3 1.1 copy-start.1
  231.7 1.6 copy-start.2
  233.3 1.1 copy-start.1
  240.8 1.6 copy-start.2
  242.3 1.1 copy-start.1
  249.8 1.6 copy-start.2
  251.4 1.1 copy-start.1
  258.8 1.6 copy-start.2
  265.1 23.5 %all-to-all-start.2 = ((bf16[512,3,4,128]{3,2,1,0:T(4,128)(2,1)}), bf16[512,3,4,128]{3,2,1,0:T(4,128)(2,1)S(1)}, u32[]{:S(2)}, u32[]{:S(2)}) async-start(bf16[512,3,4,128]{3,2,1,0:T(4,128)(2,1)} %slice_bitcast_fusion), calls=%async_computation.3 | async-start | bytes 3145728 | tf_op jit(solution)/shard_map/all_to_all | solution.py:126
Sparse Core Ops, SparseCore 0:
  9.6 119.4 all-gather.3
  138.9 42.1 reduce-scatter.1
  183.4 38.2 all-gather.5
where the time goes:
time: 299 us; the launch traced here: 298 us
  waiting for transfers between devices  199 us (67%)
  local copies, waits for them, and re-layouts  32.3 us (11%)
  matrix products  25.7 us (9%)
  other arithmetic  14.8 us (5%)
  between operations  14.5 us (5%)
  starting transfers between devices  11 us (4%)
    all_gather x1, waiting for transfers between devices, shards(): full_weight = lax.all_gather(text_weight, 'dp', axis=1, tiled=True)  121 us
    reduce_scatter x1, waiting for transfers between devices, shards(): lax.psum_scatter(lax.dot_general(full_weight, encoder_rows, (((0,), (1,))...  42.3 us
    all_to_all x1, waiting for transfers between devices, shards(): lax.all_to_all(video_local, 'seq', split_axis=2, concat_axis=0, tiled=True)  14.3 us
    all_to_all x1, waiting for transfers between devices, shards(): lax.all_to_all(video_grad, 'seq', split_axis=0, concat_axis=2, tiled=True)  13.9 us
    dot_general x1, matrix products, shards(): lax.dot_general(full_weight, encoder_rows, (((0,), (1,)), ((), ())), pref...  9.7 us
    while x2, local copies, waits for them, and re-layouts, shards(): lax.map(lambda inputs: head_grads(inputs, key_valid, block_rows, tokens),...  7.06 us
    while x28, local copies, waits for them, and re-layouts  6.83 us
  transfers between devices with their start and end apart: 6, of which 6 were waited for; matrix products, arithmetic and copies ran while one was open for 5% of the time, Pallas kernels for 0%

commit v1 on v0

v1 whole, which is shorter than its diff:
```python
import functools
import math

import jax
import jax.numpy as jnp
from jax import lax
from jax.experimental import pallas as pl
from jax.experimental.pallas import tpu as pltpu
from jax.sharding import PartitionSpec as P

EPS = 1e-06
BF = jnp.bfloat16
F32 = jnp.float32


def dot_nt(a, b):
    return lax.dot_general(a, b, (((1,), (1,)), ((), ())), preferred_element_type=F32)


def dot_nn(a, b):
    return jnp.dot(a, b, preferred_element_type=F32)


def kernel(
    seq,
    dp,
    blk,
    qkv,
    cot,
    states,
    weight,
    up_text,
    gain_q,
    gain_k,
    length,
    source,
    out,
    out_text,
    xall,
    wbuf,
    vbuf,
    pbuf,
    rbuf,
    sums,
    zbuf,
    tbuf,
    tfull,
    qn_s,
    u_s,
    dq_s,
    dk_s,
    dv_s,
    gbuf,
    x_send,
    f_send,
    x_recv,
    v_send,
    v_recv,
    r_send,
    r_recv,
    z_send,
    z_recv,
    t_send,
    t_recv,
    o_send,
    o_recv,
    l_sem,
):
    ms = lax.axis_index("seq")
    md = lax.axis_index("dp")
    heads = gain_q.shape[0]
    hd = gain_q.shape[1]
    tok = qkv.shape[1]
    tokens = seq * tok
    prompt = states.shape[0]
    part = prompt // seq
    cols = weight.shape[1]
    per = dp // seq
    width = heads * hd
    half = dp // 2
    partner = md + 1 - 2 * lax.rem(md, 2)

    def seq_peer(i):
        return lax.rem(ms + i, seq)

    def dp_peer(i):
        return lax.rem(md + i, dp)

    def remote(src, dst, send, recv, where):
        return pltpu.make_async_remote_copy(
            src_ref=src,
            dst_ref=dst,
            send_sem=send,
            recv_sem=recv,
            device_id=where,
            device_id_type=pl.DeviceIdType.MESH,
        )

    barrier = pltpu.get_barrier_semaphore()
    for i in range(1, seq):
        pl.semaphore_signal(
            barrier, inc=1, device_id={"seq": seq_peer(i)}, device_id_type=pl.DeviceIdType.MESH
        )
    for i in range(1, dp):
        pl.semaphore_signal(
            barrier, inc=1, device_id={"dp": dp_peer(i)}, device_id_type=pl.DeviceIdType.MESH
        )

    def rows_of(s):
        return pl.ds(pl.multiple_of(s * tok, tok), tok)

    def width_of(s):
        return pl.ds(pl.multiple_of(s * width, width), width)

    local_x = pltpu.make_async_copy(states, xall.at[md], l_sem.at[0])
    local_w = pltpu.make_async_copy(weight, wbuf, l_sem.at[1])
    local_v = pltpu.make_async_copy(
        qkv.at[:, :, width_of(ms)], vbuf.at[pl.ds(0, 3), rows_of(ms), :], l_sem.at[2]
    )
    local_u = pltpu.make_async_copy(
        cot.at[:, width_of(ms)], vbuf.at[3, rows_of(ms), :], l_sem.at[3]
    )
    local_x.start()
    local_w.start()
    local_v.start()
    local_u.start()
    pl.semaphore_wait(barrier, seq - 1 + dp - 1)

    def x_copy(i):
        return remote(
            states, xall.at[md], x_send.at[i], x_recv.at[md], {"dp": dp_peer(2 * i)}
        )

    def forward(g, src):
        return remote(src, xall.at[g], f_send.at[g], x_recv.at[g], {"dp": partner})

    def x_arrived(g):
        remote(states, xall.at[g], x_send.at[0], x_recv.at[g], {"dp": partner}).wait_recv()

    for i in range(1, half):
        x_copy(i).start()
    forward(md, states).start()

    def v_copy(i):
        to = seq_peer(i)
        return remote(
            qkv.at[:, :, width_of(to)],
            vbuf.at[pl.ds(0, 3), rows_of(ms), :],
            v_send.at[i, 0],
            v_recv.at[ms, 0],
            {"seq": to},
        )

    def u_copy(i):
        to = seq_peer(i)
        return remote(
            cot.at[:, width_of(to)],
            vbuf.at[3, rows_of(ms), :],
            v_send.at[i, 1],
            v_recv.at[ms, 1],
            {"seq": to},
        )

    for i in range(1, seq):
        v_copy(i).start()
        u_copy(i).start()

    for i in range(1, half):
        g = lax.rem(md + dp - 2 * i, dp)
        x_arrived(g)
        forward(g, xall.at[g]).start()
    for i in range(half):
        x_arrived(lax.rem(partner + dp - 2 * i, dp))
    local_x.wait()
    local_w.wait()

    def r_copy(c, i):
        to = seq_peer(i)
        return remote(
            pbuf.at[to, c], rbuf.at[ms, c], r_send.at[i, c], r_recv.at[ms, c], {"seq": to}
        )

    def project(n, carry):
        c = dp_peer(n)
        value = dot_nn(xall[source[c]], wbuf[...])
        for q in range(seq):
            pbuf[q, c] = value[q * part : (q + 1) * part].astype(BF)
        for i in range(1, seq):
            r_copy(c, i).start()
        return carry

    lax.fori_loop(0, dp, project, 0)

    def z_copy(c):
        return remote(sums.at[c], zbuf.at[md], z_send.at[c], z_recv.at[md], {"dp": c})

    def reduced(c):
        total = pbuf[ms, c].astype(F32)
        for i in range(1, seq):
            s = seq_peer(i)
            remote(
                pbuf.at[s, c], rbuf.at[s, c], r_send.at[i, c], r_recv.at[s, c], {"seq": s}
            ).wait_recv()
            total = total + rbuf[s, c].astype(F32)
        return total.astype(BF)

    zbuf[md] = reduced(md)

    def reduce_step(n, carry):
        c = dp_peer(n)
        sums[c] = reduced(c)
        z_copy(c).start()
        return carry

    lax.fori_loop(1, dp, reduce_step, 0)

    def z_arrived(n):
        g = dp_peer(n)
        remote(sums.at[g], zbuf.at[g], z_send.at[g], z_recv.at[g], {"dp": g}).wait_recv()

    for n in range(1, dp):
        z_arrived(dp - n)

    def t_copy(i):
        to = seq_peer(i)
        return remote(
            zbuf.at[pl.ds(to * per, per)], tbuf.at[ms], t_send.at[i], t_recv.at[ms], {"seq": to}
        )

    for i in range(1, seq):
        t_copy(i).start()
    tbuf[ms] = zbuf[pl.ds(ms * per, per)]
    for i in range(1, seq):
        s = seq_peer(i)
        remote(
            zbuf.at[pl.ds(0, per)], tbuf.at[s], t_send.at[i], t_recv.at[s], {"seq": s}
        ).wait_recv()
        remote(
            qkv.at[:, :, width_of(s)],
            vbuf.at[pl.ds(0, 3), rows_of(s), :],
            v_send.at[i, 0],
            v_recv.at[s, 0],
            {"seq": s},
        ).wait_recv()
        remote(
            cot.at[:, width_of(s)],
            vbuf.at[3, rows_of(s), :],
            v_send.at[i, 1],
            v_recv.at[s, 1],
            {"seq": s},
        ).wait_recv()
    local_v.wait()
    local_u.wait()
    for s in range(seq):
        for k in range(per):
            tfull[s * part : (s + 1) * part, k * cols : (k + 1) * cols] = tbuf[s, k].astype(F32)

    rows = tokens + prompt
    scale = 1.0 / math.sqrt(hd)
    valid = lax.broadcasted_iota(jnp.int32, (prompt, blk), 0) < length[0]

    def inverse(x):
        return lax.rsqrt(jnp.mean(x * x, axis=-1, keepdims=True) + EPS)

    def norm_back(x, r, gain, grad):
        scaled = grad * gain
        inner = jnp.mean(scaled * x, axis=-1, keepdims=True)
        return r * scaled - x * (r * r * r * inner)

    def o_copy(h, i):
        to = seq_peer(i)
        return remote(
            gbuf.at[h, :, rows_of(to), :],
            out.at[:, :, pl.ds(pl.multiple_of(ms * width + h * hd, hd), hd)],
            o_send.at[i, h],
            o_recv.at[ms, h],
            {"seq": to},
        )

    def o_local(h):
        return pltpu.make_async_copy(
            gbuf.at[h, :, rows_of(ms), :],
            out.at[:, :, pl.ds(pl.multiple_of(ms * width + h * hd, hd), hd)],
            o_send.at[0, h],
        )

    def head(h, carry):
        mine = pl.ds(pl.multiple_of(h * hd, hd), hd)

        def text_cols(j):
            return pl.ds(pl.multiple_of((h * 3 + j) * hd, hd), hd)

        def joint(j):
            return jnp.concatenate(
                [vbuf[j, :, mine].astype(F32), tfull[:, text_cols(j)]], axis=0
            )

        gq = gain_q[pl.ds(h, 1), :]
        gk = gain_k[pl.ds(h, 1), :]
        q = joint(0)
        k = joint(1)
        v = joint(2).astype(BF)
        qn_s[...] = (q * inverse(q) * gq).astype(BF)
        kn32 = (k * inverse(k) * gk).astype(BF).astype(F32)
        kn = kn32.astype(BF)
        kn_t = kn32.T.astype(BF)
        u_s[:tokens] = vbuf[3, :, mine]
        u_s[tokens:] = up_text[:, mine]

        def block(n, first):
            at = pl.ds(pl.multiple_of(n * blk, blk), blk)
            qb = qn_s[at, :]
            ub = u_s[at, :]
            e = jnp.exp2(dot_nt(kn, qb) * (scale * math.log2(math.e)))
            e = jnp.concatenate([e[:tokens], jnp.where(valid, e[tokens:], 0.0)], axis=0)
            probs = e * (1.0 / jnp.sum(e, axis=0, keepdims=True))
            grad_probs = dot_nt(v, ub)
            delta = jnp.sum(probs * grad_probs, axis=0, keepdims=True)
            grad_scores = (probs * (grad_probs - delta) * scale).astype(BF)
            dv = dot_nn(probs.astype(BF), ub)
            dk = dot_nn(grad_scores, qb)
            dq_s[at, :] = dot_nn(kn_t, grad_scores).T
            if first:
                dk_s[...] = dk
                dv_s[...] = dv
            else:
                dk_s[...] += dk
                dv_s[...] += dv

        block(0, True)
        if rows > blk:
            lax.fori_loop(1, rows // blk, lambda n, c: (block(n, False), c)[1], 0)
        grads = (
            norm_back(q, inverse(q), gq, dq_s[...]),
            norm_back(k, inverse(k), gk, dk_s[...]),
            dv_s[...],
        )
        for j in range(3):
            gbuf[h, j] = grads[j][:tokens].astype(BF)
            out_text[:, text_cols(j)] = grads[j][tokens:].astype(BF)
        for i in range(1, seq):
            o_copy(h, i).start()
        o_local(h).start()
        return carry

    lax.fori_loop(0, heads, head, 0)

    def finish(h, carry):
        o_local(h).wait()
        for i in range(1, seq):
            s = seq_peer(i)
            o_copy(h, i).wait_send()
            remote(
                gbuf.at[h, :, rows_of(s), :],
                out.at[:, :, pl.ds(pl.multiple_of(s * width + h * hd, hd), hd)],
                o_send.at[i, h],
                o_recv.at[s, h],
                {"seq": s},
            ).wait_recv()
        return carry

    lax.fori_loop(0, heads, finish, 0)

    def drain(n, carry):
        c = dp_peer(n)
        for i in range(1, seq):
            r_copy(c, i).wait_send()
        return carry

    lax.fori_loop(0, dp, drain, 0)
    for n in range(1, dp):
        z_copy(dp_peer(n)).wait_send()
    for i in range(1, half):
        x_copy(i).wait_send()
    for i in range(half):
        g = lax.rem(md + dp - 2 * i, dp)
        forward(g, xall.at[g]).wait_send()
    for i in range(1, seq):
        v_copy(i).wait_send()
        u_copy(i).wait_send()
        t_copy(i).wait_send()


def shards(
    seq,
    dp,
    video_qkv,
    video_cotangent,
    prompt_states,
    text_weight,
    text_cotangent,
    gain_query,
    gain_key,
    prompt_lengths,
    prompt_source,
):
    heads, hd = gain_query.shape
    tok = video_qkv.shape[1]
    every = video_qkv.shape[3]
    tokens = tok * seq
    prompt, feat = prompt_states.shape[1:]
    cols = text_weight.shape[1]
    part = prompt // seq
    per = dp // seq
    rows = tokens + prompt
    blk = rows if rows <= 640 else prompt
    width = heads * hd
    dma = pltpu.SemaphoreType.DMA
    hbm = pl.BlockSpec(memory_space=pl.ANY)
    vmem = pl.BlockSpec(memory_space=pltpu.VMEM)
    smem = pl.BlockSpec(memory_space=pltpu.SMEM)
    grad_video, grad_text = pl.pallas_call(
        functools.partial(kernel, seq, dp, blk),
        out_shape=(
            jax.ShapeDtypeStruct((3, tok, every), BF),
            jax.ShapeDtypeStruct((prompt, 3 * width), BF),
        ),
        in_specs=[hbm, hbm, vmem, hbm, vmem, vmem, vmem, smem, smem],
        out_specs=(hbm, vmem),
        scratch_shapes=[
            pltpu.VMEM((dp, prompt, feat), BF),
            pltpu.VMEM((feat, cols), BF),
            pltpu.VMEM((4, tokens, width), BF),
            pltpu.VMEM((seq, dp, part, cols), BF),
            pltpu.VMEM((seq, dp, part, cols), BF),
            pltpu.VMEM((dp, part, cols), BF),
            pltpu.VMEM((dp, part, cols), BF),
            pltpu.VMEM((seq, per, part, cols), BF),
            pltpu.VMEM((prompt, per * cols), F32),
            pltpu.VMEM((rows, hd), BF),
            pltpu.VMEM((rows, hd), BF),
            pltpu.VMEM((rows, hd), F32),
            pltpu.VMEM((rows, hd), F32),
            pltpu.VMEM((rows, hd), F32),
            pltpu.VMEM((heads, 3, tokens, hd), BF),
            dma((dp,)),
            dma((dp,)),
            dma((dp,)),
            dma((seq, 2)),
            dma((seq, 2)),
            dma((seq, dp)),
            dma((seq, dp)),
            dma((dp,)),
            dma((dp,)),
            dma((seq,)),
            dma((seq,)),
            dma((seq, heads)),
            dma((seq, heads)),
            dma((4,)),
        ],
        compiler_params=pltpu.CompilerParams(
            collective_id=0, has_side_effects=True, vmem_limit_bytes=56 * 1024 * 1024
        ),
    )(
        jnp.transpose(video_qkv[0], (1, 0, 2)),
        video_cotangent[0],
        prompt_states[0],
        text_weight,
        text_cotangent[0],
        gain_query,
        gain_key,
        prompt_lengths,
        prompt_source,
    )
    return jnp.transpose(grad_video, (1, 0, 2))[None], grad_text[None]


def solution(mesh):
    in_specs = (
        P("dp", "seq", None, None),
        P("dp", "seq", None),
        P("dp", None, "seq"),
        P("seq", "dp"),
        P("dp", None, "seq"),
        P("seq", None),
        P("seq", None),
        P("dp"),
        P(),
    )
    out_specs = (P("dp", "seq", None, None), P("dp", None, "seq"))
    body = functools.partial(shards, mesh.shape["seq"], mesh.shape["dp"])
    return jax.shard_map(body, mesh=mesh, in_specs=in_specs, out_specs=out_specs, check_vma=False)
```

time: 299 us -> 87.6 us (0.29)
  waiting for transfers between devices: 199 us -> 0 us
  Pallas kernels: 0 us -> 82.6 us
  local copies, waits for them, and re-layouts: 32.3 us -> 3.53 us
  matrix products: 25.7 us -> 0 us
  other arithmetic: 14.8 us -> 0 us
  between operations: 14.5 us -> 1.3 us
  starting transfers between devices: 11 us -> 0 us
    all_gather x2 -> x0, waiting for transfers between devices: 123 us -> none  [the longest x1 121 us: shards(): full_weight = lax.all_gather(text_weight, 'dp', axis=1, tiled=True)]
    pallas_call x0 -> x1, Pallas kernels: none -> 82.6 us  [shards(): pl.pallas_call(functools.partial(kernel, seq, dp, blk), out_shape=(jax.Sh...]
    reduce_scatter x1 -> x0, waiting for transfers between devices: 42.3 us -> none  [shards(): lax.psum_scatter(lax.dot_general(full_weight, encoder_rows, (((0,), (1,))...]
    all_to_all x3 -> x0, waiting for transfers between devices: 33.3 us -> none  [the longest x1 14.3 us: shards(): lax.all_to_all(video_local, 'seq', split_axis=2, concat_axis=0, tiled=True)]
    dot_general x41 -> x0, matrix products: 25.7 us -> none  [the longest x1 9.7 us: shards(): lax.dot_general(full_weight, encoder_rows, (((0,), (1,)), ((), ())), pref...]
    while x30 -> x0, local copies, waits for them, and re-layouts: 13.9 us -> none  [the longest x2 7.06 us: shards(): lax.map(lambda inputs: head_grads(inputs, key_valid, block_rows, tokens),...]
    all_to_all x3 -> x0, starting transfers between devices: 10.9 us -> none  [the longest x1 3.75 us: shards(): lax.all_to_all(video_local, 'seq', split_axis=2, concat_axis=0, tiled=True)]
    reduce_sum x9 -> x0, other arithmetic: 4.39 us -> none  [the longest x1 2.63 us: pick_block(): jnp.sum(jnp.where(hits.reshape(shape), piece, jnp.zeros_like(piece)), axi...]
  transfers between devices with their start and end apart: 6 -> 0, of which waited for: 6 -> 0; matrix products, arithmetic and copies ran while one was open for 5% -> 0% of each run, Pallas kernels for 0% -> 0%
where the time goes in v1:
time: 87.6 us; the launch traced here: 87.4 us
  Pallas kernels  82.6 us (94%)
  local copies, waits for them, and re-layouts  3.53 us (4%)
  between operations  1.3 us (1%)
    pallas_call x1, Pallas kernels, shards(): pl.pallas_call(functools.partial(kernel, seq, dp, blk), out_shape=(jax.Sh...  82.6 us
    unnamed x4, local copies, waits for them, and re-layouts  3.53 us

profile of v1, /device:TPU:0, one launch (start us, length us, event | category | flops | bytes accessed | tf_op | source)
XLA Modules:
  0.0 87.4 jit_solution(2280157300658099187)
XLA Ops:
  1.3 82.6 %shard_map.104 = (bf16[3,128,2048]{2,1,0:T(8,128)(2,1)}, bf16[128,1536]{1,0:T(8,128)(2,1)}) custom-call(bf16[3,128,2048]{2,1,0:T(8,128)(2,1)} %bitcast.11, bf16[128,2048]{1,0:T(8,128)(2,1)} %bitcast.12, bf16[128,1024]{1,0:T(8,128)(2,1)} %bitcast.14, bf16[1024,768]{1,0:T(8,128)(2,1)} %weight.1, bf16[128,512]{1,0:T(8,128)(2,1)} %bitcast.15, f32[4,128]{1,0:T(4,128)} %gain_q.1, ...), custom_call_target="tpu_custom_call" | custom-call | tf_op jit(solution)/shard_map/pallas_call | solution.py:412
  83.8 0.0 copy-start
  83.9 2.8 %copy.14 = bf16[1,128,3,2048]{3,1,2,0:T(8,128)(2,1)} copy(bf16[1,128,3,2048]{3,1,2,0:T(8,128)(2,1)} %bitcast.10) | data formatting | bytes 3145728
  86.6 0.0 copy-done
  86.6 0.7 copy.15
Async XLA Ops:
  83.8 2.8 %copy-start = (bf16[128,1536]{1,0:T(8,128)(2,1)S(1)}, bf16[128,1536]{1,0:T(8,128)(2,1)}, u32[]{:S(2)}) copy-start(bf16[128,1536]{1,0:T(8,128)(2,1)} %get-tuple-element.5) | copy-start | bytes 1179652

commit v2 on v1

--- a/solution.py
+++ b/solution.py
@@ -42,7 +42,7 @@
     pbuf,
     rbuf,
     sums,
-    zbuf,
+    zsend,
     tbuf,
     tfull,
     qn_s,
@@ -51,16 +51,17 @@
     dk_s,
     dv_s,
     gbuf,
-    x_send,
+    up_send,
+    down_send,
     f_send,
     x_recv,
     v_send,
     v_recv,
+    u_send,
+    u_recv,
     r_send,
     r_recv,
     z_send,
-    z_recv,
-    t_send,
     t_recv,
     o_send,
     o_recv,
@@ -106,151 +107,236 @@
             barrier, inc=1, device_id={"dp": dp_peer(i)}, device_id_type=pl.DeviceIdType.MESH
         )
 
+    for i in range(seq):
+        for k in range(per):
+            @pl.when((seq_peer(i) != ms) | (ms * per + k != md))
+            def _(i=i, k=k):
+                pl.semaphore_signal(
+                    barrier,
+                    inc=1,
+                    device_id={"seq": seq_peer(i), "dp": ms * per + k},
+                    device_id_type=pl.DeviceIdType.MESH,
+                )
+
     def rows_of(s):
         return pl.ds(pl.multiple_of(s * tok, tok), tok)
 
     def width_of(s):
         return pl.ds(pl.multiple_of(s * width, width), width)
 
-    local_x = pltpu.make_async_copy(states, xall.at[md], l_sem.at[0])
     local_w = pltpu.make_async_copy(weight, wbuf, l_sem.at[1])
-    local_v = pltpu.make_async_copy(
-        qkv.at[:, :, width_of(ms)], vbuf.at[pl.ds(0, 3), rows_of(ms), :], l_sem.at[2]
-    )
-    local_u = pltpu.make_async_copy(
-        cot.at[:, width_of(ms)], vbuf.at[3, rows_of(ms), :], l_sem.at[3]
-    )
-    local_x.start()
     local_w.start()
-    local_v.start()
-    local_u.start()
-    pl.semaphore_wait(barrier, seq - 1 + dp - 1)
-
-    def x_copy(i):
+    pl.semaphore_wait(barrier, seq - 1 + dp - 1 + dp - jnp.where(md // per == ms, 1, 0))
+
+    FIRST, SECOND = min(2, heads), min(3, heads)
+    core = lax.rem(md, 2)
+    place = md // 2
+
+    def hop(g, src, up):
         return remote(
-            states, xall.at[md], x_send.at[i], x_recv.at[md], {"dp": dp_peer(2 * i)}
+            src,
+            xall.at[g],
+            (up_send if up else down_send).at[g],
+            x_recv.at[g],
+            {"dp": md + 2 if up else md - 2},
         )
 
     def forward(g, src):
         return remote(src, xall.at[g], f_send.at[g], x_recv.at[g], {"dp": partner})
 
     def x_arrived(g):
-        remote(states, xall.at[g], x_send.at[0], x_recv.at[g], {"dp": partner}).wait_recv()
-
-    for i in range(1, half):
-        x_copy(i).start()
+        remote(states, xall.at[g], f_send.at[g], x_recv.at[g], {"dp": partner}).wait_recv()
+
+    @pl.when(place + 1 < half)
+    def _():
+        hop(md, states, True).start()
+
+    @pl.when(place > 0)
+    def _():
+        hop(md, states, False).start()
+
     forward(md, states).start()
 
-    def v_copy(i):
+    def head_cols(s, h):
+        return pl.ds(pl.multiple_of(s * width + h * hd, hd), hd)
+
+    def v_copy(h, i):
         to = seq_peer(i)
         return remote(
-            qkv.at[:, :, width_of(to)],
-            vbuf.at[pl.ds(0, 3), rows_of(ms), :],
-            v_send.at[i, 0],
-            v_recv.at[ms, 0],
+            qkv.at[:, :, head_cols(to, h)],
+            vbuf.at[h, pl.ds(0, 3), rows_of(ms), :],
+            v_send.at[i, h],
+            v_recv.at[ms, h],
             {"seq": to},
         )
 
-    def u_copy(i):
+    def u_copy(h, i):
         to = seq_peer(i)
         return remote(
-            cot.at[:, width_of(to)],
-            vbuf.at[3, rows_of(ms), :],
-            v_send.at[i, 1],
-            v_recv.at[ms, 1],
+            cot.at[:, head_cols(to, h)],
+            vbuf.at[h, 3, rows_of(ms), :],
+            u_send.at[i, h],
+            u_recv.at[ms, h],
             {"seq": to},
         )
 
-    for i in range(1, seq):
-        v_copy(i).start()
-        u_copy(i).start()
-
-    for i in range(1, half):
-        g = lax.rem(md + dp - 2 * i, dp)
-        x_arrived(g)
-        forward(g, xall.at[g]).start()
-    for i in range(half):
-        x_arrived(lax.rem(partner + dp - 2 * i, dp))
-    local_x.wait()
-    local_w.wait()
-
-    def r_copy(c, i):
+    def send_head(h):
+        for i in range(1, seq):
+            v_copy(h, i).start()
+            u_copy(h, i).start()
+
+    def own_qkv(h):
+        return pltpu.make_async_copy(
+            qkv.at[:, :, head_cols(ms, h)],
+            vbuf.at[h, pl.ds(0, 3), rows_of(ms), :],
+            v_send.at[0, h],
+        )
+
+    def own_cot(h):
+        return pltpu.make_async_copy(
+            cot.at[:, head_cols(ms, h)], vbuf.at[h, 3, rows_of(ms), :], u_send.at[0, h]
+        )
+
+    def head_arrived(h):
+        own_qkv(h).wait()
+        own_cot(h).wait()
+        for i in range(1, seq):
+            s = seq_peer(i)
+            remote(
+                qkv.at[:, :, head_cols(s, h)],
+                vbuf.at[h, pl.ds(0, 3), rows_of(s), :],
+                v_send.at[i, h],
+                v_recv.at[s, h],
+                {"seq": s},
+            ).wait_recv()
+            remote(
+                cot.at[:, head_cols(s, h)],
+                vbuf.at[h, 3, rows_of(s), :],
+                u_send.at[i, h],
+                u_recv.at[s, h],
+                {"seq": s},
+            ).wait_recv()
+
+    def r_copy(g, i):
         to = seq_peer(i)
         return remote(
-            pbuf.at[to, c], rbuf.at[ms, c], r_send.at[i, c], r_recv.at[ms, c], {"seq": to}
-        )
-
-    def project(n, carry):
-        c = dp_peer(n)
-        value = dot_nn(xall[source[c]], wbuf[...])
+            pbuf.at[to, g], rbuf.at[ms, g], r_send.at[i, g], r_recv.at[ms, g], {"seq": to}
+        )
+
+    def project(g, value):
+        value = dot_nn(value, wbuf[...])
         for q in range(seq):
-            pbuf[q, c] = value[q * part : (q + 1) * part].astype(BF)
-        for i in range(1, seq):
-            r_copy(c, i).start()
+            pbuf[q, g] = value[q * part : (q + 1) * part].astype(BF)
+        for i in range(1, seq):
+            r_copy(g, i).start()
+
+    local_w.wait()
+    project(md, states[...])
+    x_arrived(partner)
+    project(partner, xall[partner])
+    for h in range(FIRST):
+        send_head(h)
+
+    def step(k, carry):
+        low = place - k
+        high = place + k
+
+        @pl.when(low >= 0)
+        def _():
+            g = 2 * low + core
+            x_arrived(g)
+
+            @pl.when(place + 1 < half)
+            def _():
+                hop(g, xall.at[g], True).start()
+
+            forward(g, xall.at[g]).start()
+
+        @pl.when(high < half)
+        def _():
+            g = 2 * high + core
+            x_arrived(g)
+
+            @pl.when(place > 0)
+            def _():
+                hop(g, xall.at[g], False).start()
+
+            forward(g, xall.at[g]).start()
+
+        @pl.when(low >= 0)
+        def _():
+            g = 2 * low + core
+            project(g, xall[g])
+            x_arrived(2 * low + 1 - core)
+            project(2 * low + 1 - core, xall[2 * low + 1 - core])
+
+        @pl.when(high < half)
+        def _():
+            g = 2 * high + core
+            project(g, xall[g])
+            x_arrived(2 * high + 1 - core)
+            project(2 * high + 1 - core, xall[2 * high + 1 - core])
+
         return carry
 
-    lax.fori_loop(0, dp, project, 0)
-
-    def z_copy(c):
-        return remote(sums.at[c], zbuf.at[md], z_send.at[c], z_recv.at[md], {"dp": c})
-
-    def reduced(c):
-        total = pbuf[ms, c].astype(F32)
+    lax.fori_loop(1, half, step, 0)
+    for h in range(FIRST, SECOND):
+        send_head(h)
+
+    def reduce_step(g, carry):
+        total = pbuf[ms, g].astype(F32)
         for i in range(1, seq):
             s = seq_peer(i)
             remote(
-                pbuf.at[s, c], rbuf.at[s, c], r_send.at[i, c], r_recv.at[s, c], {"seq": s}
+                pbuf.at[s, g], rbuf.at[s, g], r_send.at[i, g], r_recv.at[s, g], {"seq": s}
             ).wait_recv()
-            total = total + rbuf[s, c].astype(F32)
-        return total.astype(BF)
-
-    zbuf[md] = reduced(md)
-
-    def reduce_step(n, carry):
+            total = total + rbuf[s, g].astype(F32)
+        sums[g] = total.astype(BF)
+        return carry
+
+    lax.fori_loop(0, dp, reduce_step, 0)
+
+    goal = md // per
+    slot = lax.rem(md, per)
+
+    def z_copy(c):
+        return remote(
+            zsend.at[c], tbuf.at[ms, slot], z_send.at[c], t_recv.at[ms, slot], {"seq": goal, "dp": c}
+        )
+
+    def z_step(n, carry):
         c = dp_peer(n)
-        sums[c] = reduced(c)
+        zsend[c] = sums[source[c]]
         z_copy(c).start()
         return carry
 
-    lax.fori_loop(1, dp, reduce_step, 0)
-
-    def z_arrived(n):
-        g = dp_peer(n)
-        remote(sums.at[g], zbuf.at[g], z_send.at[g], z_recv.at[g], {"dp": g}).wait_recv()
-
-    for n in range(1, dp):
-        z_arrived(dp - n)
-
-    def t_copy(i):
-        to = seq_peer(i)
-        return remote(
-            zbuf.at[pl.ds(to * per, per)], tbuf.at[ms], t_send.at[i], t_recv.at[ms], {"seq": to}
-        )
-
-    for i in range(1, seq):
-        t_copy(i).start()
-    tbuf[ms] = zbuf[pl.ds(ms * per, per)]
-    for i in range(1, seq):
-        s = seq_peer(i)
-        remote(
-            zbuf.at[pl.ds(0, per)], tbuf.at[s], t_send.at[i], t_recv.at[s], {"seq": s}
-        ).wait_recv()
-        remote(
-            qkv.at[:, :, width_of(s)],
-            vbuf.at[pl.ds(0, 3), rows_of(s), :],
-            v_send.at[i, 0],
-            v_recv.at[s, 0],
-            {"seq": s},
-        ).wait_recv()
-        remote(
-            cot.at[:, width_of(s)],
-            vbuf.at[3, rows_of(s), :],
-            v_send.at[i, 1],
-            v_recv.at[s, 1],
-            {"seq": s},
-        ).wait_recv()
-    local_v.wait()
-    local_u.wait()
+    lax.fori_loop(1, dp, z_step, 0)
+    zsend[md] = sums[source[md]]
+
+    @pl.when(goal == ms)
+    def _():
+        tbuf[ms, slot] = zsend[md]
+
+    @pl.when(goal != ms)
+    def _():
+        z_copy(md).start()
+
+    for h in range(SECOND, heads):
+        send_head(h)
+    for h in range(heads):
+        own_qkv(h).start()
+        own_cot(h).start()
+
+    def t_arrived(s, k):
+        @pl.when((s != ms) | (ms * per + k != md))
+        def _():
+            remote(
+                zsend.at[0], tbuf.at[s, k], z_send.at[0], t_recv.at[s, k], {"seq": seq_peer(1)}
+            ).wait_recv()
+
+    for s in range(seq):
+        for k in range(per):
+            t_arrived(s, k)
     for s in range(seq):
         for k in range(per):
             tfull[s * part : (s + 1) * part, k * cols : (k + 1) * cols] = tbuf[s, k].astype(F32)
@@ -292,9 +378,10 @@
 
         def joint(j):
             return jnp.concatenate(
-                [vbuf[j, :, mine].astype(F32), tfull[:, text_cols(j)]], axis=0
+                [vbuf[h, j].astype(F32), tfull[:, text_cols(j)]], axis=0
             )
 
+        head_arrived(h)
         gq = gain_q[pl.ds(h, 1), :]
         gk = gain_k[pl.ds(h, 1), :]
         q = joint(0)
@@ -304,7 +391,7 @@
         kn32 = (k * inverse(k) * gk).astype(BF).astype(F32)
         kn = kn32.astype(BF)
         kn_t = kn32.T.astype(BF)
-        u_s[:tokens] = vbuf[3, :, mine]
+        u_s[:tokens] = vbuf[h, 3]
         u_s[tokens:] = up_text[:, mine]
 
         def block(n, first):
@@ -361,24 +448,38 @@
 
     lax.fori_loop(0, heads, finish, 0)
 
+    def forward_wait(g):
+        @pl.when(lax.rem(g, 2) == core)
+        def _():
+            forward(g, xall.at[g]).wait_send()
+            at = g // 2
+
+            @pl.when((at <= place) & (place + 1 < half))
+            def _():
+                hop(g, xall.at[g], True).wait_send()
+
+            @pl.when((at >= place) & (place > 0))
+            def _():
+                hop(g, xall.at[g], False).wait_send()
+
     def drain(n, carry):
-        c = dp_peer(n)
-        for i in range(1, seq):
-            r_copy(c, i).wait_send()
+        for i in range(1, seq):
+            r_copy(n, i).wait_send()
+        forward_wait(n)
         return carry
 
     lax.fori_loop(0, dp, drain, 0)
     for n in range(1, dp):
         z_copy(dp_peer(n)).wait_send()
-    for i in range(1, half):
-        x_copy(i).wait_send()
-    for i in range(half):
-        g = lax.rem(md + dp - 2 * i, dp)
-        forward(g, xall.at[g]).wait_send()
+
+    @pl.when(goal != ms)
+    def _():
+        z_copy(md).wait_send()
+
     for i in range(1, seq):
-        v_copy(i).wait_send()
-        u_copy(i).wait_send()
-        t_copy(i).wait_send()
+        for h in range(heads):
+            v_copy(h, i).wait_send()
+            u_copy(h, i).wait_send()
 
 
 def shards(
@@ -420,7 +521,7 @@
         scratch_shapes=[
             pltpu.VMEM((dp, prompt, feat), BF),
             pltpu.VMEM((feat, cols), BF),
-            pltpu.VMEM((4, tokens, width), BF),
+            pltpu.VMEM((heads, 4, tokens, hd), BF),
             pltpu.VMEM((seq, dp, part, cols), BF),
             pltpu.VMEM((seq, dp, part, cols), BF),
             pltpu.VMEM((dp, part, cols), BF),
@@ -436,14 +537,15 @@
             dma((dp,)),
             dma((dp,)),
             dma((dp,)),
-            dma((seq, 2)),
-            dma((seq, 2)),
+            dma((dp,)),
+            dma((seq, heads)),
+            dma((seq, heads)),
+            dma((seq, heads)),
+            dma((seq, heads)),
             dma((seq, dp)),
             dma((seq, dp)),
             dma((dp,)),
-            dma((dp,)),
-            dma((seq,)),
-            dma((seq,)),
+            dma((seq, per)),
             dma((seq, heads)),
             dma((seq, heads)),
             dma((4,)),

time: 87.6 us -> 77.8 us (0.89)
  Pallas kernels: 82.6 us -> 72.8 us
    pallas_call x1, Pallas kernels: 82.6 us -> 72.8 us  [shards(): pl.pallas_call(functools.partial(kernel, seq, dp, blk), out_shape=(jax.Sh...]
where the time goes in v2:
time: 77.8 us; the launch traced here: 77.6 us
  Pallas kernels  72.8 us (94%)
  local copies, waits for them, and re-layouts  3.53 us (5%)
  between operations  1.3 us (2%)
    pallas_call x1, Pallas kernels, shards(): pl.pallas_call(functools.partial(kernel, seq, dp, blk), out_shape=(jax.Sh...  72.8 us
    unnamed x4, local copies, waits for them, and re-layouts  3.53 us

profile of v2, /device:TPU:0, one launch (start us, length us, event | category | flops | bytes accessed | tf_op | source)
XLA Modules:
  0.0 77.6 jit_solution(9841934848502770373)
XLA Ops:
  1.3 72.8 %shard_map.104 = (bf16[3,128,2048]{2,1,0:T(8,128)(2,1)}, bf16[128,1536]{1,0:T(8,128)(2,1)}) custom-call(bf16[3,128,2048]{2,1,0:T(8,128)(2,1)} %bitcast.11, bf16[128,2048]{1,0:T(8,128)(2,1)} %bitcast.12, bf16[128,1024]{1,0:T(8,128)(2,1)} %bitcast.14, bf16[1024,768]{1,0:T(8,128)(2,1)} %weight.1, bf16[128,512]{1,0:T(8,128)(2,1)} %bitcast.15, f32[4,128]{1,0:T(4,128)} %gain_q.1, ...), custom_call_target="tpu_custom_call" | custom-call | tf_op jit(solution)/shard_map/pallas_call | solution.py:513
  74.0 0.0 copy-start
  74.0 2.8 %copy.14 = bf16[1,128,3,2048]{3,1,2,0:T(8,128)(2,1)} copy(bf16[1,128,3,2048]{3,1,2,0:T(8,128)(2,1)} %bitcast.10) | data formatting | bytes 3145728
  76.8 0.0 copy-done
  76.8 0.7 copy.15
Async XLA Ops:
  74.0 2.8 %copy-start = (bf16[128,1536]{1,0:T(8,128)(2,1)S(1)}, bf16[128,1536]{1,0:T(8,128)(2,1)}, u32[]{:S(2)}) copy-start(bf16[128,1536]{1,0:T(8,128)(2,1)} %get-tuple-element.5) | copy-start | bytes 1179652

commit v3 on v2

--- a/solution.py
+++ b/solution.py
@@ -51,6 +51,8 @@
     dk_s,
     dv_s,
     gbuf,
+    up_s,
+    text_s,
     up_send,
     down_send,
     f_send,
@@ -66,6 +68,7 @@
     o_send,
     o_recv,
     l_sem,
+    text_sem,
 ):
     ms = lax.axis_index("seq")
     md = lax.axis_index("dp")
@@ -125,7 +128,11 @@
         return pl.ds(pl.multiple_of(s * width, width), width)
 
     local_w = pltpu.make_async_copy(weight, wbuf, l_sem.at[1])
+    local_x = pltpu.make_async_copy(states, xall.at[md], l_sem.at[0])
+    local_u = pltpu.make_async_copy(up_text, up_s, l_sem.at[2])
+    local_x.start()
     local_w.start()
+    local_u.start()
     pl.semaphore_wait(barrier, seq - 1 + dp - 1 + dp - jnp.where(md // per == ms, 1, 0))
 
     FIRST, SECOND = min(2, heads), min(3, heads)
@@ -230,8 +237,9 @@
         for i in range(1, seq):
             r_copy(g, i).start()
 
+    local_x.wait()
     local_w.wait()
-    project(md, states[...])
+    project(md, xall[md])
     x_arrived(partner)
     project(partner, xall[partner])
     for h in range(FIRST):
@@ -369,6 +377,10 @@
             out.at[:, :, pl.ds(pl.multiple_of(ms * width + h * hd, hd), hd)],
             o_send.at[0, h],
         )
+
+    def text_local(h):
+        at = pl.ds(pl.multiple_of(h * 3 * hd, 3 * hd), 3 * hd)
+        return pltpu.make_async_copy(text_s.at[:, at], out_text.at[:, at], text_sem.at[h])
 
     def head(h, carry):
         mine = pl.ds(pl.multiple_of(h * hd, hd), hd)
@@ -392,7 +404,7 @@
         kn = kn32.astype(BF)
         kn_t = kn32.T.astype(BF)
         u_s[:tokens] = vbuf[h, 3]
-        u_s[tokens:] = up_text[:, mine]
+        u_s[tokens:] = up_s[:, mine]
 
         def block(n, first):
             at = pl.ds(pl.multiple_of(n * blk, blk), blk)
@@ -424,16 +436,19 @@
         )
         for j in range(3):
             gbuf[h, j] = grads[j][:tokens].astype(BF)
-            out_text[:, text_cols(j)] = grads[j][tokens:].astype(BF)
+            text_s[:, text_cols(j)] = grads[j][tokens:].astype(BF)
         for i in range(1, seq):
             o_copy(h, i).start()
         o_local(h).start()
+        text_local(h).start()
         return carry
 
+    local_u.wait()
     lax.fori_loop(0, heads, head, 0)
 
     def finish(h, carry):
         o_local(h).wait()
+        text_local(h).wait()
         for i in range(1, seq):
             s = seq_peer(i)
             o_copy(h, i).wait_send()
@@ -480,6 +495,16 @@
         for h in range(heads):
             v_copy(h, i).wait_send()
             u_copy(h, i).wait_send()
+
+
+def hand_over(video, text, video_out, text_out, sems):
+    moves = [
+        pltpu.make_async_copy(video.at[j], video_out.at[j], sems.at[j]) for j in range(3)
+    ] + [pltpu.make_async_copy(text, text_out, sems.at[3])]
+    for move in moves:
+        move.start()
+    for move in moves:
+        move.wait()
 
 
 def shards(
@@ -516,8 +541,8 @@
             jax.ShapeDtypeStruct((3, tok, every), BF),
             jax.ShapeDtypeStruct((prompt, 3 * width), BF),
         ),
-        in_specs=[hbm, hbm, vmem, hbm, vmem, vmem, vmem, smem, smem],
-        out_specs=(hbm, vmem),
+        in_specs=[hbm, hbm, hbm, hbm, hbm, vmem, vmem, smem, smem],
+        out_specs=(hbm, hbm),
         scratch_shapes=[
             pltpu.VMEM((dp, prompt, feat), BF),
             pltpu.VMEM((feat, cols), BF),
@@ -534,6 +559,8 @@
             pltpu.VMEM((rows, hd), F32),
             pltpu.VMEM((rows, hd), F32),
             pltpu.VMEM((heads, 3, tokens, hd), BF),
+            pltpu.VMEM((prompt, width), BF),
+            pltpu.VMEM((prompt, 3 * width), BF),
             dma((dp,)),
             dma((dp,)),
             dma((dp,)),
@@ -549,6 +576,7 @@
             dma((seq, heads)),
             dma((seq, heads)),
             dma((4,)),
+            dma((heads,)),
         ],
         compiler_params=pltpu.CompilerParams(
             collective_id=0, has_side_effects=True, vmem_limit_bytes=56 * 1024 * 1024
@@ -564,6 +592,16 @@
         prompt_lengths,
         prompt_source,
     )
+    grad_video, grad_text = pl.pallas_call(
+        hand_over,
+        out_shape=(
+            jax.ShapeDtypeStruct(grad_video.shape, BF),
+            jax.ShapeDtypeStruct(grad_text.shape, BF),
+        ),
+        in_specs=[vmem, vmem],
+        out_specs=(hbm, hbm),
+        scratch_shapes=[dma((4,))],
+    )(grad_video, grad_text)
     return jnp.transpose(grad_video, (1, 0, 2))[None], grad_text[None]
 
 

time: 77.8 us -> 76 us (0.977)
  local copies, waits for them, and re-layouts: 3.53 us -> 0 us
  Pallas kernels: 72.8 us -> 74.6 us
    unnamed x4 -> x0, local copies, waits for them, and re-layouts: 3.53 us -> none
    pallas_call x0 -> x1, Pallas kernels: none -> 2.77 us  [shards(): pl.pallas_call(hand_over, out_shape=(jax.ShapeDtypeStruct(grad_video.shap...]
    pallas_call x1, Pallas kernels: 72.8 us -> 71.8 us  [shards(): pl.pallas_call(functools.partial(kernel, seq, dp, blk), out_shape=(jax.Sh...]
where the time goes in v3:
time: 76 us; the launch traced here: 75.9 us
  Pallas kernels  74.6 us (98%)
  between operations  1.29 us (2%)
    pallas_call x1, Pallas kernels, shards(): pl.pallas_call(functools.partial(kernel, seq, dp, blk), out_shape=(jax.Sh...  71.8 us
    pallas_call x1, Pallas kernels, shards(): pl.pallas_call(hand_over, out_shape=(jax.ShapeDtypeStruct(grad_video.shap...  2.77 us

profile of v3, /device:TPU:0, one launch (start us, length us, event | category | flops | bytes accessed | tf_op | source)
XLA Modules:
  0.0 75.9 jit_solution(7398075173403478527)
XLA Ops:
  1.3 71.8 %shard_map.104 = (bf16[3,128,2048]{2,1,0:T(8,128)(2,1)}, bf16[128,1536]{1,0:T(8,128)(2,1)}) custom-call(bf16[3,128,2048]{2,1,0:T(8,128)(2,1)} %bitcast.10, bf16[128,2048]{1,0:T(8,128)(2,1)} %bitcast.11, bf16[128,1024]{1,0:T(8,128)(2,1)} %bitcast.12, bf16[1024,768]{1,0:T(8,128)(2,1)} %weight.1, bf16[128,512]{1,0:T(8,128)(2,1)} %bitcast.13, f32[4,128]{1,0:T(4,128)} %gain_q.1, ...), custom_call_target="tpu_custom_call" | custom-call | tf_op jit(solution)/shard_map/pallas_call | solution.py:538
  73.1 2.8 %shard_map.105 = (bf16[3,128,2048]{2,1,0:T(8,128)(2,1)}, bf16[128,1536]{1,0:T(8,128)(2,1)}) custom-call(bf16[3,128,2048]{2,1,0:T(8,128)(2,1)} %get-tuple-element.6.video, bf16[128,1536]{1,0:T(8,128)(2,1)} %get-tuple-element.7.text), custom_call_target="tpu_custom_call" | custom-call | tf_op jit(solution)/shard_map/pallas_call | solution.py:595

commit v4 on v3

--- a/solution.py
+++ b/solution.py
@@ -237,12 +237,13 @@
         for i in range(1, seq):
             r_copy(g, i).start()
 
+    send_head(0)
     local_x.wait()
     local_w.wait()
     project(md, xall[md])
     x_arrived(partner)
     project(partner, xall[partner])
-    for h in range(FIRST):
+    for h in range(1, FIRST):
         send_head(h)
 
     def step(k, carry):

time: 76 us -> 75.9 us (level)
  no operation moved by 1% of the time
where the time goes in v4:
time: 75.9 us; the launch traced here: 75.7 us
  Pallas kernels  74.4 us (98%)
  between operations  1.29 us (2%)
    pallas_call x1, Pallas kernels, shards(): pl.pallas_call(functools.partial(kernel, seq, dp, blk), out_shape=(jax.Sh...  71.6 us
    pallas_call x1, Pallas kernels, shards(): pl.pallas_call(hand_over, out_shape=(jax.ShapeDtypeStruct(grad_video.shap...  2.77 us

profile of v4, /device:TPU:0, one launch (start us, length us, event | category | flops | bytes accessed | tf_op | source)
XLA Modules:
  0.0 75.7 jit_solution(13735957843103856405)
XLA Ops:
  1.3 71.6 %shard_map.104 = (bf16[3,128,2048]{2,1,0:T(8,128)(2,1)}, bf16[128,1536]{1,0:T(8,128)(2,1)}) custom-call(bf16[3,128,2048]{2,1,0:T(8,128)(2,1)} %bitcast.10, bf16[128,2048]{1,0:T(8,128)(2,1)} %bitcast.11, bf16[128,1024]{1,0:T(8,128)(2,1)} %bitcast.12, bf16[1024,768]{1,0:T(8,128)(2,1)} %weight.1, bf16[128,512]{1,0:T(8,128)(2,1)} %bitcast.13, f32[4,128]{1,0:T(4,128)} %gain_q.1, ...), custom_call_target="tpu_custom_call" | custom-call | tf_op jit(solution)/shard_map/pallas_call | solution.py:539
  72.9 2.8 %shard_map.105 = (bf16[3,128,2048]{2,1,0:T(8,128)(2,1)}, bf16[128,1536]{1,0:T(8,128)(2,1)}) custom-call(bf16[3,128,2048]{2,1,0:T(8,128)(2,1)} %get-tuple-element.6.video, bf16[128,1536]{1,0:T(8,128)(2,1)} %get-tuple-element.7.text), custom_call_target="tpu_custom_call" | custom-call | tf_op jit(solution)/shard_map/pallas_call | solution.py:596
